TPU v7x, 1024 devices: a whole 4x4x32 slice. The times are simulated.
1024 devices in a mesh: slab: 32 (over z), grp: 32 (over y, x, core).
Axes of the slice: x: 4, y: 4, z: 32, core: 2. Of those that a mesh axis runs over, the one named last changes fastest.
Arguments:
- multipoles: bfloat16 [32, 32768, 128], P('grp', 'slab'), may hold values from -6 to 6
- translations: float32 [16, 128, 128], replicated, may hold values from -0.5 to 0.5
- m2l_list: int32 [3, 32, 131072], P(None, 'grp', 'slab'), may hold values from 0 to 1023, as said below
- send_counts: int32 [32, 1024], P('grp', 'slab'), may hold values from 1 to 128, as said below
- positions: float32 [32, 3, 16384], P('grp', None, 'slab'), may hold values from 0 to 1
- charges: float32 [32, 16384], P('grp', 'slab'), may hold values from -0.3 to 0.3
- leaf_counts: int32 [32, 32], P('grp', 'slab'), may hold values from 64 to 512, as said below
- particle_cell: int32 [32, 16384], P('grp', 'slab'), may hold values from 0 to 1023
- basis: bfloat16 [32, 128, 16384], P('grp', None, 'slab'), may hold values from -0.1875 to 0.1875
Outputs:
- local_exp: float32 [32, 32768, 128], P('grp', 'slab')
- potential: float32 [32, 16384], P('grp', 'slab')
Inputs may be any that keep to these rules, and one draw needn't show every extreme that they name: `m2l_list`: slot k * 128 + j of a device holds an entry for the peer at slab index k of its group: row 0 a target cell among the device's own 1024 cells, row 1 a source cell among that peer's 1024 cells, row 2 an offset id below 16. Only slots with j below the matching send count are read. `send_counts`: entry k of a device counts the rows that the peer at slab index k of its group sends to it (its used slots for that peer). In every group one device sends 128 rows to every device of the group, and every device receives 128 rows from some peer. `leaf_counts`: some device holds 512 live particles.
All inputs are finite; a program needn't handle non-finite values.
Results may differ from a plain program's by a relative error of at most 0.0003.
Values may be sent and summed in bfloat16 or wider, within the bound.
No kernel may reach another device: no remote copies, remote signals or barrier semaphores. Data moves between devices by JAX's collectives and lax.ppermute only.
A program may use at most 64 MiB of HBM per device.

v0:
```python
import functools

import jax
import jax.numpy as jnp
from jax import lax
from jax.experimental import pallas as pl
from jax.experimental.pallas import tpu as pltpu
from jax.sharding import PartitionSpec as P

SOFT = 0.01
SLABS = 32
STRIDE = 4
EARLY = (0, 1, -1, 2, -2)
ORDER = (*EARLY, 3, -3, 4)
RELAYED = {1: ORDER, -1: ORDER, 2: (0, 1, 2, 3), -2: (0, -1, -2, -3)}
VMEM_BYTES = 56 * 1024 * 1024


def shifted(value, amount):
    count = lax.axis_size("slab")
    pairs = [(i, (i + amount) % count) for i in range(count)]
    return lax.ppermute(value, "slab", pairs)


def ask_kernel(me_ref, list_ref, *outs):
    for out, (relay, ks) in zip(outs, RELAYED.items(), strict=True):
        for i, k in enumerate(ks):
            out[pl.ds(i, 1), :] = list_ref[1, pl.ds(peer(me_ref[0], relay, k), 1), :]


def peer(me, relay, k):
    return lax.rem(me + (relay + STRIDE * k + SLABS), SLABS)


def ask(me, lists):
    return pl.pallas_call(
        ask_kernel,
        out_shape=[jax.ShapeDtypeStruct((len(ks), lists.shape[2]), jnp.int32) for ks in RELAYED.values()],
        in_specs=[pl.BlockSpec(memory_space=pltpu.SMEM), pl.BlockSpec(memory_space=pltpu.VMEM)],
        out_specs=[pl.BlockSpec(memory_space=pltpu.VMEM)] * len(RELAYED),
    )(me, lists)


def table_kernel(matrix_ref, out_ref):
    for o in range(matrix_ref.shape[0]):
        turned = matrix_ref[o].T
        high = turned.astype(jnp.bfloat16)
        out_ref[0:128, o * 128 : (o + 1) * 128] = high
        rest = turned - high.astype(jnp.float32)
        out_ref[128:256, o * 128 : (o + 1) * 128] = rest.astype(jnp.bfloat16)


def split_table(translations):
    return pl.pallas_call(
        table_kernel,
        out_shape=jax.ShapeDtypeStruct((256, translations.shape[0] * 128), jnp.bfloat16),
        in_specs=[pl.BlockSpec(memory_space=pltpu.VMEM)],
        out_specs=pl.BlockSpec(memory_space=pltpu.VMEM),
        compiler_params=pltpu.CompilerParams(vmem_limit_bytes=VMEM_BYTES),
    )(translations)


def pack_kernel(plan, known, me_ref, list_ref, *refs):
    asked = dict(zip(RELAYED, refs[: len(RELAYED)], strict=True))
    refs = refs[len(RELAYED) :]
    count = len(RELAYED) + 1
    before = refs[:count] if known else ()
    blocks, outs = refs[len(before) : -count], refs[-count:]
    for k, parts, uses in plan:
        if k in known:
            for relay, slot in uses:
                dest = 0 if relay == 0 else 1 + list(RELAYED).index(relay)
                outs[dest][slot] = before[dest][kept(known, relay).index(k)]
            continue
        lists = []
        for relay, _ in uses:
            if relay == 0:
                lists.append(list_ref[1, pl.ds(peer(me_ref[0], 0, k), 1), :])
            else:
                lists.append(asked[relay][pl.ds(RELAYED[relay].index(k), 1), :])
        wanted = jnp.concatenate(lists, axis=1)
        total = None
        for ref, base in parts:
            block = blocks[ref][...]
            place = lax.broadcasted_iota(jnp.int32, (block.shape[0], wanted.shape[1]), 0)
            pick = jnp.where(place + base == wanted, 1.0, 0.0).astype(jnp.bfloat16)
            part = lax.dot_general(
                block, pick, (((0,), (0,)), ((), ())), preferred_element_type=jnp.float32
            )
            total = part if total is None else total + part
        rows = total.astype(jnp.bfloat16)
        for i, (relay, slot) in enumerate(uses):
            dest = 0 if relay == 0 else 1 + list(RELAYED).index(relay)
            outs[dest][slot] = rows[:, i * 128 : (i + 1) * 128]


def kept(names, relay):
    return [k for k in names if relay == 0 or k in RELAYED[relay]]


def pack(parts, blocks, me, lists, asked, known=(), before=()):
    relays = [0, *RELAYED]
    plan = []
    for k in parts:
        uses = [(r, kept(parts, r).index(k)) for r in relays if r == 0 or k in RELAYED[r]]
        plan.append((k, parts[k], uses))
    sizes = [len(kept(parts, r)) for r in relays]
    return pl.pallas_call(
        functools.partial(pack_kernel, plan, known),
        out_shape=[jax.ShapeDtypeStruct((size, 128, 128), jnp.bfloat16) for size in sizes],
        in_specs=[pl.BlockSpec(memory_space=pltpu.SMEM)]
        + [pl.BlockSpec(memory_space=pltpu.VMEM)] * (1 + len(asked) + len(before) + len(blocks)),
        out_specs=[pl.BlockSpec(memory_space=pltpu.VMEM)] * len(sizes),
        compiler_params=pltpu.CompilerParams(vmem_limit_bytes=VMEM_BYTES),
        cost_estimate=pl.CostEstimate(
            flops=2 * 4096 * 512 * 128, bytes_accessed=2 * 1024 * 1024, transcendentals=0
        ),
    )(me, lists, *asked, *before, *blocks)


def translate_kernel(groups, me_ref, count_ref, live_ref, table_ref, list_ref, near_ref, cell_ref, basis_ref, *refs):
    rows, out_ref, potential_ref, total = refs[:-3], refs[-3], refs[-2], refs[-1]
    cells, slots = out_ref.shape[1], near_ref.shape[1]
    offsets = table_ref.shape[1] // 128
    lane = lax.broadcasted_iota(jnp.int32, (1, 128), 1)
    for n, group in enumerate(groups):
        taken = jnp.concatenate([rows[a][b] for a, b, _, _ in group], axis=1)
        targets, kinds = [], []
        for _, _, relay, k in group:
            at = peer(me_ref[0], relay, k)
            targets.append(list_ref[0, pl.ds(at, 1), :])
            kinds.append(jnp.where(lane < count_ref[at], list_ref[2, pl.ds(at, 1), :], -1))
        target = jnp.concatenate(targets, axis=1)
        kind = jnp.concatenate(kinds, axis=1)
        spread = jnp.concatenate(
            [taken * jnp.where(kind == o, 1.0, 0.0).astype(jnp.bfloat16) for o in range(offsets)],
            axis=0,
        )
        both = jnp.dot(table_ref[...], spread, preferred_element_type=jnp.float32)
        pair = split(both[:128] + both[128:], 0)
        place = lax.broadcasted_iota(jnp.int32, (cells, target.shape[1]), 0)
        pick = jnp.where(place == target, 1.0, 0.0).astype(jnp.bfloat16)
        part = lax.dot_general(
            pick, pair, (((1,), (1,)), ((), ())), preferred_element_type=jnp.float32
        )
        if n == 0:
            total[...] = part
        else:
            total[...] += part
    local = total[:, :128] + total[:, 128:]
    out_ref[0] = local
    place = lax.broadcasted_iota(jnp.int32, (cells, slots), 0)
    pick = jnp.where(place == cell_ref[...], 1.0, 0.0).astype(jnp.bfloat16)
    both = lax.dot_general(
        split(local, 1), pick, (((0,), (0,)), ((), ())), preferred_element_type=jnp.float32
    )
    far = jnp.sum((both[:128] + both[128:]) * basis_ref[...].astype(jnp.float32), axis=0, keepdims=True)
    slot = lax.broadcasted_iota(jnp.int32, (1, slots), 1)
    potential_ref[...] = jnp.where(slot < live_ref[0], near_ref[...] + far, 0.0)


def split(value, axis):
    high = value.astype(jnp.bfloat16)
    low = (value - high.astype(jnp.float32)).astype(jnp.bfloat16)
    return jnp.concatenate([high, low], axis=axis)


def translate(me, counts, table, lists, parts, cells, near, live, cell, basis):
    flat = [(a, b, relay, k) for a, (_, relay, ks) in enumerate(parts) for b, k in enumerate(ks)]
    groups = [flat[i : i + 4] for i in range(0, len(flat), 4)]
    return pl.pallas_call(
        functools.partial(translate_kernel, groups),
        out_shape=(
            jax.ShapeDtypeStruct((1, cells, 128), jnp.float32),
            jax.ShapeDtypeStruct(near.shape, jnp.float32),
        ),
        in_specs=[pl.BlockSpec(memory_space=pltpu.SMEM)] * 3
        + [pl.BlockSpec(memory_space=pltpu.VMEM)] * (5 + len(parts)),
        out_specs=[pl.BlockSpec(memory_space=pltpu.VMEM)] * 2,
        scratch_shapes=[pltpu.VMEM((cells, 256), jnp.float32)],
        compiler_params=pltpu.CompilerParams(vmem_limit_bytes=VMEM_BYTES),
        cost_estimate=pl.CostEstimate(
            flops=2 * len(flat) * 128 * 256 * (table.shape[1] + cells),
            bytes_accessed=len(flat) * 32768 + 2 * cells * 512,
            transcendentals=0,
        ),
    )(me, counts, live, table, lists, near, cell, basis, *[part for part, _, _ in parts])


def extended(block, axis):
    count = lax.axis_size(axis)
    forward = [(i, i + 1) for i in range(count - 1)]
    backward = [(target, source) for source, target in forward]
    return [lax.ppermute(block, axis, forward), block, lax.ppermute(block, axis, backward)]


def pair_sum(targets, sources):
    dist = (targets[0][:, None] - sources[0][None, :]) ** 2
    dist = dist + (targets[1][:, None] - sources[1][None, :]) ** 2
    dist = dist + (targets[2][:, None] - sources[2][None, :]) ** 2
    return jnp.sum(sources[3][None, :] / jnp.sqrt(dist + SOFT), axis=1)


def shards(
    multipoles,
    translations,
    m2l_list,
    send_counts,
    positions,
    charges,
    leaf_counts,
    particle_cell,
    basis,
):
    cells_dev = multipoles.shape[1]
    part_dev = charges.shape[1]
    me = lax.axis_index("slab").astype(jnp.int32).reshape(1)
    lists = m2l_list.reshape(3, SLABS, m2l_list.shape[2] // SLABS)
    counts = send_counts[0]

    asked = [shifted(value, relay) for value, relay in zip(ask(me, lists), RELAYED, strict=True)]

    chain = {0: multipoles[0]}
    for k in (1, 2, 3):
        chain[-k] = shifted(chain[1 - k], STRIDE)
        chain[k] = shifted(chain[k - 1], -STRIDE)
    live = jnp.arange(part_dev, dtype=jnp.int32) < leaf_counts[0, 0]
    masked = jnp.where(live, charges[0], 0.0)
    stacked = jnp.concatenate([positions[0], masked[None, :]], axis=0)
    near = sum(pair_sum(positions[0], sources) for sources in extended(stacked, "grp"))
    near = jnp.where(live, near, 0.0)[None, :]
    table = split_table(translations)
    early = pack({k: [(i, 0)] for i, k in enumerate(EARLY)}, [chain[k] for k in EARLY], me, lists, asked)
    up, down = chain[-3], chain[3]
    asked, early, near, table = lax.optimization_barrier((asked, early, near, table))

    middle = cells_dev // 2
    ends = [shifted(up[:middle], STRIDE), shifted(down[middle:], -STRIDE)]
    places = {k: [] for k in EARLY}
    places |= {3: [(0, 0)], -3: [(1, 0)], 4: [(2, 0), (3, middle)]}
    packed = pack(places, [down, up, *ends], me, lists, asked, EARLY, early)
    parts = [(packed[0], 0, ORDER)]
    for value, (relay, ks) in zip(packed[1:], RELAYED.items(), strict=True):
        parts.append((shifted(value, -relay), relay, ks))
    return translate(
        me, counts, table, lists, parts, cells_dev, near, leaf_counts[0], particle_cell, basis[0]
    )


def solution(mesh):
    placed = (
        P("grp", "slab", None),
        P(),
        P(None, "grp", "slab"),
        P("grp", "slab"),
        P("grp", None, "slab"),
        P("grp", "slab"),
        P("grp", "slab"),
        P("grp", "slab"),
        P("grp", None, "slab"),
    )
    return jax.shard_map(
        shards,
        mesh=mesh,
        in_specs=placed,
        out_specs=(P("grp", "slab", None), P("grp", "slab")),
        check_vma=False,
    )
```

profile of v0, /device:TPU:1, one launch (start us, length us, event | category | flops | bytes accessed | tf_op | source)
XLA Modules:
  0.0 161.8 jit_solution(14608224188080560718)
XLA Ops:
  0.6 9.6 %collective-permute-start.5 = (bf16[1024,128]{1,0:T(8,128)(2,1)}, bf16[1024,128]{1,0:T(8,128)(2,1)S(1)}, u32[]{:S(2)}, u32[]{:S(2)}) collective-permute-start(bf16[1024,128]{1,0:T(8,128)(2,1)} %bitcast.44), channel_id=1, source_target_pairs={{0,128},{32,160},{64,192},{96,224},{128,256},{160,288},{192,320},{... | collective-permute-start | bytes 786440 | tf_op jit(solution)/shard_map/ppermute | solution.py:22
  10.3 12.8 %collective-permute-start.4 = (bf16[1024,128]{1,0:T(8,128)(2,1)}, bf16[1024,128]{1,0:T(8,128)(2,1)S(1)}, u32[]{:S(2)}, u32[]{:S(2)}) collective-permute-start(bf16[1024,128]{1,0:T(8,128)(2,1)} %bitcast.45), channel_id=1, source_target_pairs={{0,896},{32,928},{64,960},{96,992},{128,0},{160,32},{192,64},{224,... | collective-permute-start | bytes 786440 | tf_op jit(solution)/shard_map/ppermute | solution.py:22
  24.5 3.3 %collective-permute-start.9 = (f32[4,512]{1,0:T(4,128)S(1)}, f32[4,512]{1,0:T(4,128)S(1)}, u32[]{:S(2)}, u32[]{:S(2)}) collective-permute-start(f32[4,512]{1,0:T(4,128)S(1)} %pad_maximum_fusion), channel_id=1, source_target_pairs={{1,0},{2,1},{3,2},{4,3},{5,4},{6,5},{7,6},{8,7},{9,8},{10,9},{11,1... | collective-permute-start | bytes 24584 | tf_op jit(solution)/shard_map/ppermute | solution.py:194
  27.9 2.5 %collective-permute-start.8 = (f32[4,512]{1,0:T(4,128)S(1)}, f32[4,512]{1,0:T(4,128)S(1)}, u32[]{:S(2)}, u32[]{:S(2)}) collective-permute-start(f32[4,512]{1,0:T(4,128)S(1)} %pad_maximum_fusion), channel_id=1, source_target_pairs={{0,1},{1,2},{2,3},{3,4},{4,5},{5,6},{6,7},{7,8},{8,9},{9,10},{10,1... | collective-permute-start | bytes 24584 | tf_op jit(solution)/shard_map/ppermute | solution.py:194
  31.9 3.1 %collective-permute-start.2 = (s32[4,128]{1,0:T(4,128)}, s32[4,128]{1,0:T(4,128)S(1)}, u32[]{:S(2)}, u32[]{:S(2)}) collective-permute-start(s32[4,128]{1,0:T(4,128)} %get-tuple-element.29), channel_id=1, source_target_pairs={{0,64},{32,96},{64,128},{96,160},{128,192},{160,224},{192,256},{22... | collective-permute-start | bytes 6152 | tf_op jit(solution)/shard_map/ppermute | solution.py:22
  35.0 2.5 %shard_map.106.table_ref = bf16[256,2048]{1,0:T(8,128)(2,1)} custom-call(f32[16,128,128]{2,1,0:T(8,128)} %matrix_ref.1), custom_call_target="tpu_custom_call" | custom-call | tf_op jit(solution)/shard_map/pallas_call | solution.py:54
  37.5 5.5 %collective-permute-start.3 = (s32[4,128]{1,0:T(4,128)S(1)}, s32[4,128]{1,0:T(4,128)S(1)}, u32[]{:S(2)}, u32[]{:S(2)}) collective-permute-start(s32[4,128]{1,0:T(4,128)S(1)} %copy-done.20), channel_id=1, source_target_pairs={{0,960},{32,992},{64,0},{96,32},{128,64},{160,96},{192,128},{224,1... | collective-permute-start | bytes 6152 | tf_op jit(solution)/shard_map/ppermute | solution.py:22
  43.1 1.9 %collective-permute-start.7 = (bf16[1024,128]{1,0:T(8,128)(2,1)S(1)}, bf16[1024,128]{1,0:T(8,128)(2,1)S(1)}, u32[]{:S(2)}, u32[]{:S(2)}) collective-permute-start(bf16[1024,128]{1,0:T(8,128)(2,1)S(1)} %collective-permute-done.5.refs_6_), channel_id=1, source_target_pairs={{0,128},{32,160},{64,192},{96,224},{128,256},{160,288},{192,320},{... | collective-permute-start | bytes 786440 | tf_op jit(solution)/shard_map/ppermute | solution.py:22
  45.0 8.9 %collective-permute-start.6 = (bf16[1024,128]{1,0:T(8,128)(2,1)S(1)}, bf16[1024,128]{1,0:T(8,128)(2,1)S(1)}, u32[]{:S(2)}, u32[]{:S(2)}) collective-permute-start(bf16[1024,128]{1,0:T(8,128)(2,1)S(1)} %collective-permute-done.4.refs_5_), channel_id=1, source_target_pairs={{0,896},{32,928},{64,960},{96,992},{128,0},{160,32},{192,64},{224,... | collective-permute-start | bytes 786440 | tf_op jit(solution)/shard_map/ppermute | solution.py:22
  55.9 11.8 %collective-permute-done.7.refs_8_ = bf16[1024,128]{1,0:T(8,128)(2,1)S(1)} collective-permute-done((bf16[1024,128]{1,0:T(8,128)(2,1)S(1)}, bf16[1024,128]{1,0:T(8,128)(2,1)S(1)}, u32[]{:S(2)}, u32[]{:S(2)}) %collective-permute-start.7) | collective-permute-done | bytes 262176 | tf_op jit(solution)/shard_map/ppermute | solution.py:22
  69.6 6.0 %collective-permute-done.6.refs_7_ = bf16[1024,128]{1,0:T(8,128)(2,1)S(1)} collective-permute-done((bf16[1024,128]{1,0:T(8,128)(2,1)S(1)}, bf16[1024,128]{1,0:T(8,128)(2,1)S(1)}, u32[]{:S(2)}, u32[]{:S(2)}) %collective-permute-start.6) | collective-permute-done | bytes 262176 | tf_op jit(solution)/shard_map/ppermute | solution.py:22
  75.7 7.2 %collective-permute-start.10 = (bf16[1024,128]{1,0:T(8,128)(2,1)S(1)}, bf16[1024,128]{1,0:T(8,128)(2,1)S(1)}, u32[]{:S(2)}, u32[]{:S(2)}) collective-permute-start(bf16[1024,128]{1,0:T(8,128)(2,1)S(1)} %collective-permute-done.6.refs_7_), channel_id=1, source_target_pairs={{0,896},{32,928},{64,960},{96,992},{128,0},{160,32},{192,64},{224,... | collective-permute-start | bytes 786440 | tf_op jit(solution)/shard_map/ppermute | solution.py:22
  84.4 10.5 %collective-permute-done.11.refs_10_ = bf16[1024,128]{1,0:T(8,128)(2,1)S(1)} collective-permute-done((bf16[1024,128]{1,0:T(8,128)(2,1)S(1)}, bf16[1024,128]{1,0:T(8,128)(2,1)S(1)}, u32[]{:S(2)}, u32[]{:S(2)}) %collective-permute-start.11) | collective-permute-done | bytes 262176 | tf_op jit(solution)/shard_map/ppermute | solution.py:22
  96.8 8.2 %collective-permute-done.10.refs_9_ = bf16[1024,128]{1,0:T(8,128)(2,1)S(1)} collective-permute-done((bf16[1024,128]{1,0:T(8,128)(2,1)S(1)}, bf16[1024,128]{1,0:T(8,128)(2,1)S(1)}, u32[]{:S(2)}, u32[]{:S(2)}) %collective-permute-start.10) | collective-permute-done | bytes 262176 | tf_op jit(solution)/shard_map/ppermute | solution.py:22
  107.0 7.3 %collective-permute-start.13 = (bf16[512,128]{1,0:T(8,128)(2,1)S(1)}, bf16[512,128]{1,0:T(8,128)(2,1)S(1)}, u32[]{:S(2)}, u32[]{:S(2)}) collective-permute-start(bf16[512,128]{1,0:T(8,128)(2,1)S(1)} %slice.73), channel_id=1, source_target_pairs={{0,896},{32,928},{64,960},{96,992},{128,0},{160,32},{192,64},{224,... | collective-permute-start | bytes 393224 | tf_op jit(solution)/shard_map/ppermute | solution.py:22
  116.0 3.4 %shard_map.105 = (bf16[5,128,128]{2,1,0:T(8,128)(2,1)}, bf16[5,128,128]{2,1,0:T(8,128)(2,1)}, bf16[5,128,128]{2,1,0:T(8,128)(2,1)}, bf16[3,128,128]{2,1,0:T(8,128)(2,1)}, bf16[3,128,128]{2,1,0:T(8,128)(2,1)}) custom-call(s32[1]{0:T(128)} %bitcast.me_ref, s32[3,32,128]{2,1,0:T(8,128)} %bitcast.27, s32[8,128]{1,0:T(8,128)} %copy-done.16, s32[8,128]{1,0:T(8,128)} %copy-done.17, ...), custom_call_target="tpu_custom_call" | custom-call | flops 536870912 | bytes 2097152 | tf_op jit(solution)/shard_map/pallas_call | solution.py:108
  119.4 3.6 %collective-permute-done.12.refs_11_ = bf16[512,128]{1,0:T(8,128)(2,1)S(1)} collective-permute-done((bf16[512,128]{1,0:T(8,128)(2,1)S(1)}, bf16[512,128]{1,0:T(8,128)(2,1)S(1)}, u32[]{:S(2)}, u32[]{:S(2)}) %collective-permute-start.12) | collective-permute-done | bytes 131104 | tf_op jit(solution)/shard_map/ppermute | solution.py:22
  124.3 3.0 %shard_map.107 = (bf16[8,128,128]{2,1,0:T(8,128)(2,1)}, bf16[8,128,128]{2,1,0:T(8,128)(2,1)}, bf16[8,128,128]{2,1,0:T(8,128)(2,1)}, bf16[4,128,128]{2,1,0:T(8,128)(2,1)}, bf16[4,128,128]{2,1,0:T(8,128)(2,1)}) custom-call(s32[1]{0:T(128)} %bitcast.me_ref, s32[3,32,128]{2,1,0:T(8,128)} %bitcast.28, s32[8,128]{1,0:T(8,128)} %copy-done.16, s32[8,128]{1,0:T(8,128)} %copy-done.17, ...), custom_call_target="tpu_custom_call" | custom-call | flops 536870912 | bytes 2097152 | tf_op jit(solution)/shard_map/pallas_call | solution.py:108
  127.3 3.7 %collective-permute-start.14 = (bf16[8,128,128]{2,1,0:T(8,128)(2,1)}, bf16[8,128,128]{2,1,0:T(8,128)(2,1)S(1)}, u32[]{:S(2)}, u32[]{:S(2)}) collective-permute-start(bf16[8,128,128]{2,1,0:T(8,128)(2,1)} %get-tuple-element.48), channel_id=1, source_target_pairs={{0,992},{32,0},{64,32},{96,64},{128,96},{160,128},{192,160},{224,1... | collective-permute-start | bytes 786440 | tf_op jit(solution)/shard_map/ppermute | solution.py:22
  133.0 7.0 %collective-permute-start.16 = (bf16[4,128,128]{2,1,0:T(8,128)(2,1)}, bf16[4,128,128]{2,1,0:T(8,128)(2,1)S(1)}, u32[]{:S(2)}, u32[]{:S(2)}) collective-permute-start(bf16[4,128,128]{2,1,0:T(8,128)(2,1)} %get-tuple-element.50), channel_id=1, source_target_pairs={{0,960},{32,992},{64,0},{96,32},{128,64},{160,96},{192,128},{224,1... | collective-permute-start | bytes 393224 | tf_op jit(solution)/shard_map/ppermute | solution.py:22
  140.0 3.1 %collective-permute-start.17 = (bf16[4,128,128]{2,1,0:T(8,128)(2,1)}, bf16[4,128,128]{2,1,0:T(8,128)(2,1)S(1)}, u32[]{:S(2)}, u32[]{:S(2)}) collective-permute-start(bf16[4,128,128]{2,1,0:T(8,128)(2,1)} %get-tuple-element.51), channel_id=1, source_target_pairs={{0,64},{32,96},{64,128},{96,160},{128,192},{160,224},{192,256},{22... | collective-permute-start | bytes 393224 | tf_op jit(solution)/shard_map/ppermute | solution.py:22
  143.1 4.5 %collective-permute-done.16.refs_3_ = bf16[4,128,128]{2,1,0:T(8,128)(2,1)S(1)} collective-permute-done((bf16[4,128,128]{2,1,0:T(8,128)(2,1)}, bf16[4,128,128]{2,1,0:T(8,128)(2,1)S(1)}, u32[]{:S(2)}, u32[]{:S(2)}) %collective-permute-start.16) | collective-permute-done | bytes 131104 | tf_op jit(solution)/shard_map/ppermute | solution.py:22
  147.6 3.1 %collective-permute-done.17.refs_4_ = bf16[4,128,128]{2,1,0:T(8,128)(2,1)S(1)} collective-permute-done((bf16[4,128,128]{2,1,0:T(8,128)(2,1)}, bf16[4,128,128]{2,1,0:T(8,128)(2,1)S(1)}, u32[]{:S(2)}, u32[]{:S(2)}) %collective-permute-start.17) | collective-permute-done | bytes 131104 | tf_op jit(solution)/shard_map/ppermute | solution.py:22
  151.5 10.2 %shard_map.108 = (f32[1,1024,128]{2,1,0:T(8,128)}, f32[1,512]{1,0:T(1,128)}) custom-call(s32[1]{0:T(128)} %bitcast.me_ref, s32[32]{0:T(128)} %bitcast.48, s32[1]{0:T(128)} %bitcast.23.live_ref, bf16[256,2048]{1,0:T(8,128)(2,1)} %shard_map.106.table_ref, s32[3,32,128]{2,1,0:T(8,128)} %bitcast.29, f32[1,512]{1,0:T(1,128)} %compare_select_fusion.near_ref, ...), custom_call_target="tpu_custom_call" | custom-call | flops 6442450944 | bytes 2097152 | tf_op jit(solution)/shard_map/pallas_call | solution.py:171
  (70 shorter events, 17.1 us)
Async XLA Ops:
  0.6 42.4 %collective-permute-start.5 = (bf16[1024,128]{1,0:T(8,128)(2,1)}, bf16[1024,128]{1,0:T(8,128)(2,1)S(1)}, u32[]{:S(2)}, u32[]{:S(2)}) collective-permute-start(bf16[1024,128]{1,0:T(8,128)(2,1)} %bitcast.44), channel_id=1, source_target_pairs={{0,128},{32,160},{64,192},{96,224},{128,256},{160,288},{192,320},{... | collective-permute-start | bytes 786440 | tf_op jit(solution)/shard_map/ppermute | solution.py:22
  10.3 34.7 %collective-permute-start.4 = (bf16[1024,128]{1,0:T(8,128)(2,1)}, bf16[1024,128]{1,0:T(8,128)(2,1)S(1)}, u32[]{:S(2)}, u32[]{:S(2)}) collective-permute-start(bf16[1024,128]{1,0:T(8,128)(2,1)} %bitcast.45), channel_id=1, source_target_pairs={{0,896},{32,928},{64,960},{96,992},{128,0},{160,32},{192,64},{224,... | collective-permute-start | bytes 786440 | tf_op jit(solution)/shard_map/ppermute | solution.py:22
  24.5 13.0 %collective-permute-start.9 = (f32[4,512]{1,0:T(4,128)S(1)}, f32[4,512]{1,0:T(4,128)S(1)}, u32[]{:S(2)}, u32[]{:S(2)}) collective-permute-start(f32[4,512]{1,0:T(4,128)S(1)} %pad_maximum_fusion), channel_id=1, source_target_pairs={{1,0},{2,1},{3,2},{4,3},{5,4},{6,5},{7,6},{8,7},{9,8},{10,9},{11,1... | collective-permute-start | bytes 24584 | tf_op jit(solution)/shard_map/ppermute | solution.py:194
  27.9 26.1 %collective-permute-start.8 = (f32[4,512]{1,0:T(4,128)S(1)}, f32[4,512]{1,0:T(4,128)S(1)}, u32[]{:S(2)}, u32[]{:S(2)}) collective-permute-start(f32[4,512]{1,0:T(4,128)S(1)} %pad_maximum_fusion), channel_id=1, source_target_pairs={{0,1},{1,2},{2,3},{3,4},{4,5},{5,6},{6,7},{7,8},{8,9},{9,10},{10,1... | collective-permute-start | bytes 24584 | tf_op jit(solution)/shard_map/ppermute | solution.py:194
  31.9 75.1 %collective-permute-start.2 = (s32[4,128]{1,0:T(4,128)}, s32[4,128]{1,0:T(4,128)S(1)}, u32[]{:S(2)}, u32[]{:S(2)}) collective-permute-start(s32[4,128]{1,0:T(4,128)} %get-tuple-element.29), channel_id=1, source_target_pairs={{0,64},{32,96},{64,128},{96,160},{128,192},{160,224},{192,256},{22... | collective-permute-start | bytes 6152 | tf_op jit(solution)/shard_map/ppermute | solution.py:22
  37.5 16.4 %copy-start.15 = (s32[8,128]{1,0:T(8,128)S(1)}, s32[8,128]{1,0:T(8,128)}, u32[]{:S(2)}) copy-start(s32[8,128]{1,0:T(8,128)} %get-tuple-element.27) | copy-start | bytes 12292
  37.5 77.3 %collective-permute-start.3 = (s32[4,128]{1,0:T(4,128)S(1)}, s32[4,128]{1,0:T(4,128)S(1)}, u32[]{:S(2)}, u32[]{:S(2)}) collective-permute-start(s32[4,128]{1,0:T(4,128)S(1)} %copy-done.20), channel_id=1, source_target_pairs={{0,960},{32,992},{64,0},{96,32},{128,64},{160,96},{192,128},{224,1... | collective-permute-start | bytes 6152 | tf_op jit(solution)/shard_map/ppermute | solution.py:22
  43.0 41.3 %copy-start.4 = (bf16[1024,128]{1,0:T(8,128)(2,1)}, bf16[1024,128]{1,0:T(8,128)(2,1)S(1)}, u32[]{:S(2)}) copy-start(bf16[1024,128]{1,0:T(8,128)(2,1)S(1)} %collective-permute-done.5.refs_6_) | copy-start | bytes 786436
  43.1 24.6 %collective-permute-start.7 = (bf16[1024,128]{1,0:T(8,128)(2,1)S(1)}, bf16[1024,128]{1,0:T(8,128)(2,1)S(1)}, u32[]{:S(2)}, u32[]{:S(2)}) collective-permute-start(bf16[1024,128]{1,0:T(8,128)(2,1)S(1)} %collective-permute-done.5.refs_6_), channel_id=1, source_target_pairs={{0,128},{32,160},{64,192},{96,224},{128,256},{160,288},{192,320},{... | collective-permute-start | bytes 786440 | tf_op jit(solution)/shard_map/ppermute | solution.py:22
  45.0 39.3 %copy-start.5 = (bf16[1024,128]{1,0:T(8,128)(2,1)}, bf16[1024,128]{1,0:T(8,128)(2,1)S(1)}, u32[]{:S(2)}) copy-start(bf16[1024,128]{1,0:T(8,128)(2,1)S(1)} %collective-permute-done.4.refs_5_) | copy-start | bytes 786436
  45.0 30.7 %collective-permute-start.6 = (bf16[1024,128]{1,0:T(8,128)(2,1)S(1)}, bf16[1024,128]{1,0:T(8,128)(2,1)S(1)}, u32[]{:S(2)}, u32[]{:S(2)}) collective-permute-start(bf16[1024,128]{1,0:T(8,128)(2,1)S(1)} %collective-permute-done.4.refs_5_), channel_id=1, source_target_pairs={{0,896},{32,928},{64,960},{96,992},{128,0},{160,32},{192,64},{224,... | collective-permute-start | bytes 786440 | tf_op jit(solution)/shard_map/ppermute | solution.py:22
  53.9 60.9 %collective-permute-start = (s32[8,128]{1,0:T(8,128)S(1)}, s32[8,128]{1,0:T(8,128)S(1)}, u32[]{:S(2)}, u32[]{:S(2)}) collective-permute-start(s32[8,128]{1,0:T(8,128)S(1)} %copy-done.15), channel_id=1, source_target_pairs={{0,32},{32,64},{64,96},{96,128},{128,160},{160,192},{192,224},{224... | collective-permute-start | bytes 12296 | tf_op jit(solution)/shard_map/ppermute | solution.py:22
  67.7 16.7 %copy-start.6 = (bf16[1024,128]{1,0:T(8,128)(2,1)}, bf16[1024,128]{1,0:T(8,128)(2,1)S(1)}, u32[]{:S(2)}) copy-start(bf16[1024,128]{1,0:T(8,128)(2,1)S(1)} %collective-permute-done.7.refs_8_) | copy-start | bytes 786436
  67.7 27.2 %collective-permute-start.11 = (bf16[1024,128]{1,0:T(8,128)(2,1)S(1)}, bf16[1024,128]{1,0:T(8,128)(2,1)S(1)}, u32[]{:S(2)}, u32[]{:S(2)}) collective-permute-start(bf16[1024,128]{1,0:T(8,128)(2,1)S(1)} %collective-permute-done.7.refs_8_), channel_id=1, source_target_pairs={{0,128},{32,160},{64,192},{96,224},{128,256},{160,288},{192,320},{... | collective-permute-start | bytes 786440 | tf_op jit(solution)/shard_map/ppermute | solution.py:22
  75.7 29.3 %collective-permute-start.10 = (bf16[1024,128]{1,0:T(8,128)(2,1)S(1)}, bf16[1024,128]{1,0:T(8,128)(2,1)S(1)}, u32[]{:S(2)}, u32[]{:S(2)}) collective-permute-start(bf16[1024,128]{1,0:T(8,128)(2,1)S(1)} %collective-permute-done.6.refs_7_), channel_id=1, source_target_pairs={{0,896},{32,928},{64,960},{96,992},{128,0},{160,32},{192,64},{224,... | collective-permute-start | bytes 786440 | tf_op jit(solution)/shard_map/ppermute | solution.py:22
  94.9 12.1 %copy-start = (bf16[1024,128]{1,0:T(8,128)(2,1)}, bf16[1024,128]{1,0:T(8,128)(2,1)S(1)}, u32[]{:S(2)}) copy-start(bf16[1024,128]{1,0:T(8,128)(2,1)S(1)} %collective-permute-done.11.refs_10_) | copy-start | bytes 786436
  94.9 20.0 %collective-permute-start.1 = (s32[8,128]{1,0:T(8,128)S(1)}, s32[8,128]{1,0:T(8,128)S(1)}, u32[]{:S(2)}, u32[]{:S(2)}) collective-permute-start(s32[8,128]{1,0:T(8,128)S(1)} %copy-done.14), channel_id=1, source_target_pairs={{0,992},{32,0},{64,32},{96,64},{128,96},{160,128},{192,160},{224,1... | collective-permute-start | bytes 12296 | tf_op jit(solution)/shard_map/ppermute | solution.py:22
  105.0 14.4 %copy-start.1 = (bf16[1024,128]{1,0:T(8,128)(2,1)}, bf16[1024,128]{1,0:T(8,128)(2,1)S(1)}, u32[]{:S(2)}) copy-start(bf16[1024,128]{1,0:T(8,128)(2,1)S(1)} %collective-permute-done.10.refs_9_) | copy-start | bytes 786436
  105.0 18.0 %collective-permute-start.12 = (bf16[512,128]{1,0:T(8,128)(2,1)S(1)}, bf16[512,128]{1,0:T(8,128)(2,1)S(1)}, u32[]{:S(2)}, u32[]{:S(2)}) collective-permute-start(bf16[512,128]{1,0:T(8,128)(2,1)S(1)} %slice.72), channel_id=1, source_target_pairs={{0,128},{32,160},{64,192},{96,224},{128,256},{160,288},{192,320},{... | collective-permute-start | bytes 393224 | tf_op jit(solution)/shard_map/ppermute | solution.py:22
  107.0 16.0 %collective-permute-start.13 = (bf16[512,128]{1,0:T(8,128)(2,1)S(1)}, bf16[512,128]{1,0:T(8,128)(2,1)S(1)}, u32[]{:S(2)}, u32[]{:S(2)}) collective-permute-start(bf16[512,128]{1,0:T(8,128)(2,1)S(1)} %slice.73), channel_id=1, source_target_pairs={{0,896},{32,928},{64,960},{96,992},{128,0},{160,32},{192,64},{224,... | collective-permute-start | bytes 393224 | tf_op jit(solution)/shard_map/ppermute | solution.py:22
  127.3 23.4 %collective-permute-start.14 = (bf16[8,128,128]{2,1,0:T(8,128)(2,1)}, bf16[8,128,128]{2,1,0:T(8,128)(2,1)S(1)}, u32[]{:S(2)}, u32[]{:S(2)}) collective-permute-start(bf16[8,128,128]{2,1,0:T(8,128)(2,1)} %get-tuple-element.48), channel_id=1, source_target_pairs={{0,992},{32,0},{64,32},{96,64},{128,96},{160,128},{192,160},{224,1... | collective-permute-start | bytes 786440 | tf_op jit(solution)/shard_map/ppermute | solution.py:22
  131.0 19.7 %collective-permute-start.15 = (bf16[8,128,128]{2,1,0:T(8,128)(2,1)}, bf16[8,128,128]{2,1,0:T(8,128)(2,1)S(1)}, u32[]{:S(2)}, u32[]{:S(2)}) collective-permute-start(bf16[8,128,128]{2,1,0:T(8,128)(2,1)} %get-tuple-element.49), channel_id=1, source_target_pairs={{0,32},{32,64},{64,96},{96,128},{128,160},{160,192},{192,224},{224... | collective-permute-start | bytes 786440 | tf_op jit(solution)/shard_map/ppermute | solution.py:22
  133.0 14.6 %collective-permute-start.16 = (bf16[4,128,128]{2,1,0:T(8,128)(2,1)}, bf16[4,128,128]{2,1,0:T(8,128)(2,1)S(1)}, u32[]{:S(2)}, u32[]{:S(2)}) collective-permute-start(bf16[4,128,128]{2,1,0:T(8,128)(2,1)} %get-tuple-element.50), channel_id=1, source_target_pairs={{0,960},{32,992},{64,0},{96,32},{128,64},{160,96},{192,128},{224,1... | collective-permute-start | bytes 393224 | tf_op jit(solution)/shard_map/ppermute | solution.py:22
  140.0 10.7 %collective-permute-start.17 = (bf16[4,128,128]{2,1,0:T(8,128)(2,1)}, bf16[4,128,128]{2,1,0:T(8,128)(2,1)S(1)}, u32[]{:S(2)}, u32[]{:S(2)}) collective-permute-start(bf16[4,128,128]{2,1,0:T(8,128)(2,1)} %get-tuple-element.51), channel_id=1, source_target_pairs={{0,64},{32,96},{64,128},{96,160},{128,192},{160,224},{192,256},{22... | collective-permute-start | bytes 393224 | tf_op jit(solution)/shard_map/ppermute | solution.py:22
  (15 other events, 43.3 us)
where the time goes:
time: 163 us; the launch traced here: 162 us
  starting transfers between devices  85.7 us (53%)
  waiting for transfers between devices  47.7 us (29%)
  Pallas kernels  20.6 us (13%)
  local copies, waits for them, and re-layouts  4.07 us (2%)
  other arithmetic  2.04 us (1%)
  between operations  1.68 us (1%)
    ppermute x16, starting transfers between devices, shifted(): return lax.ppermute(value, 'slab', pairs)  79.8 us
    ppermute x16, waiting for transfers between devices, shifted(): return lax.ppermute(value, 'slab', pairs)  47.7 us
    pallas_call x1, Pallas kernels, translate(): pl.pallas_call(functools.partial(translate_kernel, groups), out_shape=(ja...  10.2 us
    pallas_call x2, Pallas kernels, pack(): pl.pallas_call(functools.partial(pack_kernel, plan, known), out_shape=[ja...  6.4 us
    unnamed x43, local copies, waits for them, and re-layouts  4.02 us
    ppermute x1, starting transfers between devices, extended(): lax.ppermute(block, axis, backward)  3.33 us
  transfers between devices with their start and end apart: 18, of which 7 were waited for; matrix products, arithmetic and copies ran while one was open for 2% of the time, Pallas kernels for 5%

commit v1 on v0

--- a/solution.py
+++ b/solution.py
@@ -10,8 +10,9 @@
 SOFT = 0.01
 SLABS = 32
 STRIDE = 4
-EARLY = (0, 1, -1, 2, -2)
-ORDER = (*EARLY, 3, -3, 4)
+EARLY = (0, 1, -1, 2, -2, 3, -3)
+LATE = (4,)
+ORDER = EARLY + LATE
 RELAYED = {1: ORDER, -1: ORDER, 2: (0, 1, 2, 3), -2: (0, -1, -2, -3)}
 VMEM_BYTES = 56 * 1024 * 1024
 
@@ -118,9 +119,8 @@
     )(me, lists, *asked, *before, *blocks)
 
 
-def translate_kernel(groups, me_ref, count_ref, live_ref, table_ref, list_ref, near_ref, cell_ref, basis_ref, *refs):
-    rows, out_ref, potential_ref, total = refs[:-3], refs[-3], refs[-2], refs[-1]
-    cells, slots = out_ref.shape[1], near_ref.shape[1]
+def translate_kernel(groups, me_ref, count_ref, table_ref, list_ref, rows, total):
+    cells = total.shape[0]
     offsets = table_ref.shape[1] // 128
     lane = lax.broadcasted_iota(jnp.int32, (1, 128), 1)
     for n, group in enumerate(groups):
@@ -147,7 +147,21 @@
             total[...] = part
         else:
             total[...] += part
-    local = total[:, :128] + total[:, 128:]
+    return total[:, :128] + total[:, 128:]
+
+
+def first_kernel(groups, me_ref, count_ref, table_ref, list_ref, *refs):
+    rows, out_ref, total = refs[:-2], refs[-2], refs[-1]
+    out_ref[...] = translate_kernel(groups, me_ref, count_ref, table_ref, list_ref, rows, total)
+
+
+def last_kernel(
+    groups, me_ref, count_ref, live_ref, table_ref, list_ref, start_ref, near_ref, cell_ref, basis_ref, *refs
+):
+    rows, out_ref, potential_ref, total = refs[:-3], refs[-3], refs[-2], refs[-1]
+    cells, slots = out_ref.shape[1], near_ref.shape[1]
+    local = translate_kernel(groups, me_ref, count_ref, table_ref, list_ref, rows, total)
+    local = local + start_ref[...]
     out_ref[0] = local
     place = lax.broadcasted_iota(jnp.int32, (cells, slots), 0)
     pick = jnp.where(place == cell_ref[...], 1.0, 0.0).astype(jnp.bfloat16)
@@ -165,18 +179,27 @@
     return jnp.concatenate([high, low], axis=axis)
 
 
-def translate(me, counts, table, lists, parts, cells, near, live, cell, basis):
+def translate(me, counts, table, lists, parts, cells, last=None):
     flat = [(a, b, relay, k) for a, (_, relay, ks) in enumerate(parts) for b, k in enumerate(ks)]
     groups = [flat[i : i + 4] for i in range(0, len(flat), 4)]
-    return pl.pallas_call(
-        functools.partial(translate_kernel, groups),
-        out_shape=(
+    if last is None:
+        body, scalars, arrays = first_kernel, [me, counts], [table, lists]
+        shapes = jax.ShapeDtypeStruct((cells, 128), jnp.float32)
+        outs = pl.BlockSpec(memory_space=pltpu.VMEM)
+    else:
+        start, near, live, cell, basis = last
+        body, scalars, arrays = last_kernel, [me, counts, live], [table, lists, start, near, cell, basis]
+        shapes = [
             jax.ShapeDtypeStruct((1, cells, 128), jnp.float32),
             jax.ShapeDtypeStruct(near.shape, jnp.float32),
-        ),
-        in_specs=[pl.BlockSpec(memory_space=pltpu.SMEM)] * 3
-        + [pl.BlockSpec(memory_space=pltpu.VMEM)] * (5 + len(parts)),
-        out_specs=[pl.BlockSpec(memory_space=pltpu.VMEM)] * 2,
+        ]
+        outs = [pl.BlockSpec(memory_space=pltpu.VMEM)] * 2
+    return pl.pallas_call(
+        functools.partial(body, groups),
+        out_shape=shapes,
+        in_specs=[pl.BlockSpec(memory_space=pltpu.SMEM)] * len(scalars)
+        + [pl.BlockSpec(memory_space=pltpu.VMEM)] * (len(arrays) + len(parts)),
+        out_specs=outs,
         scratch_shapes=[pltpu.VMEM((cells, 256), jnp.float32)],
         compiler_params=pltpu.CompilerParams(vmem_limit_bytes=VMEM_BYTES),
         cost_estimate=pl.CostEstimate(
@@ -184,7 +207,7 @@
             bytes_accessed=len(flat) * 32768 + 2 * cells * 512,
             transcendentals=0,
         ),
-    )(me, counts, live, table, lists, near, cell, basis, *[part for part, _, _ in parts])
+    )(*scalars, *arrays, *[part for part, _, _ in parts])
 
 
 def extended(block, axis):
@@ -220,31 +243,42 @@
 
     asked = [shifted(value, relay) for value, relay in zip(ask(me, lists), RELAYED, strict=True)]
 
-    chain = {0: multipoles[0]}
+    middle = cells_dev // 2
+    chain = {0: (multipoles[0],)}
     for k in (1, 2, 3):
-        chain[-k] = shifted(chain[1 - k], STRIDE)
-        chain[k] = shifted(chain[k - 1], -STRIDE)
+        if k == 2:
+            sides = {key: (chain[key][0][:middle], chain[key][0][middle:]) for key in (1 - k, k - 1)}
+        else:
+            sides = chain
+        chain[-k] = tuple(shifted(part, STRIDE) for part in sides[1 - k])
+        chain[k] = tuple(shifted(part, -STRIDE) for part in reversed(sides[k - 1]))[::-1]
+    chain[4] = (shifted(chain[-3][0], STRIDE), shifted(chain[3][1], -STRIDE))
+
     live = jnp.arange(part_dev, dtype=jnp.int32) < leaf_counts[0, 0]
     masked = jnp.where(live, charges[0], 0.0)
     stacked = jnp.concatenate([positions[0], masked[None, :]], axis=0)
     near = sum(pair_sum(positions[0], sources) for sources in extended(stacked, "grp"))
     near = jnp.where(live, near, 0.0)[None, :]
     table = split_table(translations)
-    early = pack({k: [(i, 0)] for i, k in enumerate(EARLY)}, [chain[k] for k in EARLY], me, lists, asked)
-    up, down = chain[-3], chain[3]
+    def places(names):
+        spots, flat = {}, []
+        for k in names:
+            spots[k] = []
+            for part, base in zip(chain[k], (0, middle), strict=False):
+                spots[k].append((len(flat), base))
+                flat.append(part)
+        return spots, flat
+
+    early = pack(*places(EARLY), me, lists, asked)
     asked, early, near, table = lax.optimization_barrier((asked, early, near, table))
-
-    middle = cells_dev // 2
-    ends = [shifted(up[:middle], STRIDE), shifted(down[middle:], -STRIDE)]
-    places = {k: [] for k in EARLY}
-    places |= {3: [(0, 0)], -3: [(1, 0)], 4: [(2, 0), (3, middle)]}
-    packed = pack(places, [down, up, *ends], me, lists, asked, EARLY, early)
-    parts = [(packed[0], 0, ORDER)]
+    spots, flat = places(LATE)
+    packed = pack({k: [] for k in EARLY} | spots, flat, me, lists, asked, EARLY, early)
+    parts = []
     for value, (relay, ks) in zip(packed[1:], RELAYED.items(), strict=True):
         parts.append((shifted(value, -relay), relay, ks))
-    return translate(
-        me, counts, table, lists, parts, cells_dev, near, leaf_counts[0], particle_cell, basis[0]
-    )
+    add = functools.partial(translate, me, counts, table, lists)
+    start = add([(packed[0], 0, ORDER)], cells_dev)
+    return add(parts, cells_dev, (start, near, leaf_counts[0], particle_cell, basis[0]))
 
 
 def solution(mesh):

time: 163 us -> 157 us (0.963)
  the two profiles are of different devices: /device:TPU:1 before, /device:TPU:32 now
where the time goes in v1:
time: 157 us; the launch traced here: 156 us
  starting transfers between devices  102 us (65%)
  Pallas kernels  24.1 us (15%)
  waiting for transfers between devices  22 us (14%)
  local copies, waits for them, and re-layouts  4.94 us (3%)
  other arithmetic  2.03 us (1%)
  between operations  1.81 us (1%)
    ppermute x20, starting transfers between devices, shifted(): return lax.ppermute(value, 'slab', pairs)  97.2 us
    ppermute x20, waiting for transfers between devices, shifted(): return lax.ppermute(value, 'slab', pairs)  22 us
    pallas_call x2, Pallas kernels, translate(): pl.pallas_call(functools.partial(body, groups), out_shape=shapes, in_spec...  13.5 us
    pallas_call x2, Pallas kernels, pack(): pl.pallas_call(functools.partial(pack_kernel, plan, known), out_shape=[ja...  6.6 us
    unnamed x51, local copies, waits for them, and re-layouts  4.88 us
  transfers between devices with their start and end apart: 22, of which 6 were waited for; matrix products, arithmetic and copies ran while one was open for 1% of the time, Pallas kernels for 8%

profile of v1, /device:TPU:32, one launch (start us, length us, event | category | flops | bytes accessed | tf_op | source)
XLA Modules:
  0.0 156.5 jit_solution(9456325504570568092)
XLA Ops:
  3.3 3.0 %collective-permute-start.14 = (f32[4,512]{1,0:T(4,128)S(1)}, f32[4,512]{1,0:T(4,128)S(1)}, u32[]{:S(2)}, u32[]{:S(2)}) collective-permute-start(f32[4,512]{1,0:T(4,128)S(1)} %pad_maximum_fusion), channel_id=1, source_target_pairs={{0,1},{1,2},{2,3},{3,4},{4,5},{5,6},{6,7},{7,8},{8,9},{9,10},{10,1... | collective-permute-start | bytes 24584 | tf_op jit(solution)/shard_map/ppermute | solution.py:217
  6.4 9.1 %collective-permute-start.5 = (bf16[1024,128]{1,0:T(8,128)(2,1)}, bf16[1024,128]{1,0:T(8,128)(2,1)S(1)}, u32[]{:S(2)}, u32[]{:S(2)}) collective-permute-start(bf16[1024,128]{1,0:T(8,128)(2,1)} %bitcast.45), channel_id=1, source_target_pairs={{0,128},{32,160},{64,192},{96,224},{128,256},{160,288},{192,320},{... | collective-permute-start | bytes 786440 | tf_op jit(solution)/shard_map/ppermute | solution.py:23
  15.5 11.9 %collective-permute-start.4 = (bf16[1024,128]{1,0:T(8,128)(2,1)}, bf16[1024,128]{1,0:T(8,128)(2,1)S(1)}, u32[]{:S(2)}, u32[]{:S(2)}) collective-permute-start(bf16[1024,128]{1,0:T(8,128)(2,1)} %bitcast.46), channel_id=1, source_target_pairs={{0,896},{32,928},{64,960},{96,992},{128,0},{160,32},{192,64},{224,... | collective-permute-start | bytes 786440 | tf_op jit(solution)/shard_map/ppermute | solution.py:23
  28.9 3.4 %collective-permute-start.2 = (s32[4,128]{1,0:T(4,128)}, s32[4,128]{1,0:T(4,128)S(1)}, u32[]{:S(2)}, u32[]{:S(2)}) collective-permute-start(s32[4,128]{1,0:T(4,128)} %get-tuple-element.29), channel_id=1, source_target_pairs={{0,64},{32,96},{64,128},{96,160},{128,192},{160,224},{192,256},{22... | collective-permute-start | bytes 6152 | tf_op jit(solution)/shard_map/ppermute | solution.py:23
  32.3 2.6 %shard_map.106.table_ref = bf16[256,2048]{1,0:T(8,128)(2,1)} custom-call(f32[16,128,128]{2,1,0:T(8,128)} %matrix_ref.1), custom_call_target="tpu_custom_call" | custom-call | tf_op jit(solution)/shard_map/pallas_call | solution.py:55
  34.8 5.6 %collective-permute-start.3 = (s32[4,128]{1,0:T(4,128)S(1)}, s32[4,128]{1,0:T(4,128)S(1)}, u32[]{:S(2)}, u32[]{:S(2)}) collective-permute-start(s32[4,128]{1,0:T(4,128)S(1)} %copy-done.24), channel_id=1, source_target_pairs={{0,960},{32,992},{64,0},{96,32},{128,64},{160,96},{192,128},{224,1... | collective-permute-start | bytes 6152 | tf_op jit(solution)/shard_map/ppermute | solution.py:23
  43.6 5.4 %collective-permute-start.8 = (bf16[512,128]{1,0:T(8,128)(2,1)S(1)}, bf16[512,128]{1,0:T(8,128)(2,1)S(1)}, u32[]{:S(2)}, u32[]{:S(2)}) collective-permute-start(bf16[512,128]{1,0:T(8,128)(2,1)S(1)} %get-tuple-element.56), channel_id=1, source_target_pairs={{0,128},{32,160},{64,192},{96,224},{128,256},{160,288},{192,320},{... | collective-permute-start | bytes 393224 | tf_op jit(solution)/shard_map/ppermute | solution.py:23
  49.0 2.1 %collective-permute-done.4.refs_5_ = bf16[1024,128]{1,0:T(8,128)(2,1)S(1)} collective-permute-done((bf16[1024,128]{1,0:T(8,128)(2,1)}, bf16[1024,128]{1,0:T(8,128)(2,1)S(1)}, u32[]{:S(2)}, u32[]{:S(2)}) %collective-permute-start.4) | collective-permute-done | bytes 262176 | tf_op jit(solution)/shard_map/ppermute | solution.py:23
  51.8 8.4 %collective-permute-start.7 = (bf16[512,128]{1,0:T(8,128)(2,1)S(1)}, bf16[512,128]{1,0:T(8,128)(2,1)S(1)}, u32[]{:S(2)}, u32[]{:S(2)}) collective-permute-start(bf16[512,128]{1,0:T(8,128)(2,1)S(1)} %get-tuple-element.57), channel_id=1, source_target_pairs={{0,896},{32,928},{64,960},{96,992},{128,0},{160,32},{192,64},{224,... | collective-permute-start | bytes 393224 | tf_op jit(solution)/shard_map/ppermute | solution.py:23
  63.6 7.8 %collective-permute-start.6 = (bf16[512,128]{1,0:T(8,128)(2,1)S(1)}, bf16[512,128]{1,0:T(8,128)(2,1)S(1)}, u32[]{:S(2)}, u32[]{:S(2)}) collective-permute-start(bf16[512,128]{1,0:T(8,128)(2,1)S(1)} %get-tuple-element.58), channel_id=1, source_target_pairs={{0,896},{32,928},{64,960},{96,992},{128,0},{160,32},{192,64},{224,... | collective-permute-start | bytes 393224 | tf_op jit(solution)/shard_map/ppermute | solution.py:23
  73.4 7.8 %collective-permute-start.11 = (bf16[512,128]{1,0:T(8,128)(2,1)S(1)}, bf16[512,128]{1,0:T(8,128)(2,1)S(1)}, u32[]{:S(2)}, u32[]{:S(2)}) collective-permute-start(bf16[512,128]{1,0:T(8,128)(2,1)S(1)} %collective-permute-done.7.refs_8_), channel_id=1, source_target_pairs={{0,896},{32,928},{64,960},{96,992},{128,0},{160,32},{192,64},{224,... | collective-permute-start | bytes 393224 | tf_op jit(solution)/shard_map/ppermute | solution.py:23
  85.8 5.8 %collective-permute-done.6.refs_7_ = bf16[512,128]{1,0:T(8,128)(2,1)S(1)} collective-permute-done((bf16[512,128]{1,0:T(8,128)(2,1)S(1)}, bf16[512,128]{1,0:T(8,128)(2,1)S(1)}, u32[]{:S(2)}, u32[]{:S(2)}) %collective-permute-start.6) | collective-permute-done | bytes 131104 | tf_op jit(solution)/shard_map/ppermute | solution.py:23
  91.7 2.0 %collective-permute-start.10 = (bf16[512,128]{1,0:T(8,128)(2,1)S(1)}, bf16[512,128]{1,0:T(8,128)(2,1)S(1)}, u32[]{:S(2)}, u32[]{:S(2)}) collective-permute-start(bf16[512,128]{1,0:T(8,128)(2,1)S(1)} %collective-permute-done.6.refs_7_), channel_id=1, source_target_pairs={{0,896},{32,928},{64,960},{96,992},{128,0},{160,32},{192,64},{224,... | collective-permute-start | bytes 393224 | tf_op jit(solution)/shard_map/ppermute | solution.py:23
  93.7 9.0 %collective-permute-start.16 = (bf16[512,128]{1,0:T(8,128)(2,1)S(1)}, bf16[512,128]{1,0:T(8,128)(2,1)S(1)}, u32[]{:S(2)}, u32[]{:S(2)}) collective-permute-start(bf16[512,128]{1,0:T(8,128)(2,1)S(1)} %collective-permute-done.12.refs_13_), channel_id=1, source_target_pairs={{0,128},{32,160},{64,192},{96,224},{128,256},{160,288},{192,320},{... | collective-permute-start | bytes 393224 | tf_op jit(solution)/shard_map/ppermute | solution.py:23
  105.3 9.6 %collective-permute-done.10.refs_11_ = bf16[512,128]{1,0:T(8,128)(2,1)S(1)} collective-permute-done((bf16[512,128]{1,0:T(8,128)(2,1)S(1)}, bf16[512,128]{1,0:T(8,128)(2,1)S(1)}, u32[]{:S(2)}, u32[]{:S(2)}) %collective-permute-start.10) | collective-permute-done | bytes 131104 | tf_op jit(solution)/shard_map/ppermute | solution.py:23
  115.6 4.0 %shard_map.105 = (bf16[7,128,128]{2,1,0:T(8,128)(2,1)}, bf16[7,128,128]{2,1,0:T(8,128)(2,1)}, bf16[7,128,128]{2,1,0:T(8,128)(2,1)}, bf16[4,128,128]{2,1,0:T(8,128)(2,1)}, bf16[4,128,128]{2,1,0:T(8,128)(2,1)}) custom-call(s32[1]{0:T(128)} %bitcast.me_ref, s32[3,32,128]{2,1,0:T(8,128)} %bitcast.27, s32[8,128]{1,0:T(8,128)} %copy-done.18, s32[8,128]{1,0:T(8,128)} %copy-done.21, ...), custom_call_target="tpu_custom_call" | custom-call | flops 536870912 | bytes 2097152 | tf_op jit(solution)/shard_map/pallas_call | solution.py:109
  121.1 2.6 %shard_map.107 = (bf16[8,128,128]{2,1,0:T(8,128)(2,1)}, bf16[8,128,128]{2,1,0:T(8,128)(2,1)}, bf16[8,128,128]{2,1,0:T(8,128)(2,1)}, bf16[4,128,128]{2,1,0:T(8,128)(2,1)}, bf16[4,128,128]{2,1,0:T(8,128)(2,1)}) custom-call(s32[1]{0:T(128)} %bitcast.me_ref, s32[3,32,128]{2,1,0:T(8,128)} %bitcast.28, s32[8,128]{1,0:T(8,128)} %copy-done.18, s32[8,128]{1,0:T(8,128)} %copy-done.21, ...), custom_call_target="tpu_custom_call" | custom-call | flops 536870912 | bytes 2097152 | tf_op jit(solution)/shard_map/pallas_call | solution.py:109
  123.7 3.7 %collective-permute-start.18 = (bf16[8,128,128]{2,1,0:T(8,128)(2,1)}, bf16[8,128,128]{2,1,0:T(8,128)(2,1)S(1)}, u32[]{:S(2)}, u32[]{:S(2)}) collective-permute-start(bf16[8,128,128]{2,1,0:T(8,128)(2,1)} %get-tuple-element.48), channel_id=1, source_target_pairs={{0,992},{32,0},{64,32},{96,64},{128,96},{160,128},{192,160},{224,1... | collective-permute-start | bytes 786440 | tf_op jit(solution)/shard_map/ppermute | solution.py:23
  127.4 2.2 %collective-permute-start.19 = (bf16[8,128,128]{2,1,0:T(8,128)(2,1)}, bf16[8,128,128]{2,1,0:T(8,128)(2,1)S(1)}, u32[]{:S(2)}, u32[]{:S(2)}) collective-permute-start(bf16[8,128,128]{2,1,0:T(8,128)(2,1)} %get-tuple-element.49), channel_id=1, source_target_pairs={{0,32},{32,64},{64,96},{96,128},{128,160},{160,192},{192,224},{224... | collective-permute-start | bytes 786440 | tf_op jit(solution)/shard_map/ppermute | solution.py:23
  129.6 7.2 %collective-permute-start.20 = (bf16[4,128,128]{2,1,0:T(8,128)(2,1)}, bf16[4,128,128]{2,1,0:T(8,128)(2,1)S(1)}, u32[]{:S(2)}, u32[]{:S(2)}) collective-permute-start(bf16[4,128,128]{2,1,0:T(8,128)(2,1)} %get-tuple-element.50), channel_id=1, source_target_pairs={{0,960},{32,992},{64,0},{96,32},{128,64},{160,96},{192,128},{224,1... | collective-permute-start | bytes 393224 | tf_op jit(solution)/shard_map/ppermute | solution.py:23
  136.8 2.1 %collective-permute-start.21 = (bf16[4,128,128]{2,1,0:T(8,128)(2,1)}, bf16[4,128,128]{2,1,0:T(8,128)(2,1)S(1)}, u32[]{:S(2)}, u32[]{:S(2)}) collective-permute-start(bf16[4,128,128]{2,1,0:T(8,128)(2,1)} %get-tuple-element.51), channel_id=1, source_target_pairs={{0,64},{32,96},{64,128},{96,160},{128,192},{160,224},{192,256},{22... | collective-permute-start | bytes 393224 | tf_op jit(solution)/shard_map/ppermute | solution.py:23
  138.9 4.8 %shard_map.108.start_ref = f32[1024,128]{1,0:T(8,128)} custom-call(s32[1]{0:T(128)} %bitcast.me_ref, s32[32]{0:T(128)} %bitcast.49, bf16[256,2048]{1,0:T(8,128)(2,1)} %shard_map.106.table_ref, s32[3,32,128]{2,1,0:T(8,128)} %bitcast.29, bf16[8,128,128]{2,1,0:T(8,128)(2,1)} %get-tuple-element.46.refs_0_), custom_call_target="tpu_custom_call" | custom-call | flops 1610612736 | bytes 1310720 | tf_op jit(solution)/shard_map/pallas_call | solution.py:197
  143.7 3.2 %collective-permute-done.21.refs_3_ = bf16[4,128,128]{2,1,0:T(8,128)(2,1)S(1)} collective-permute-done((bf16[4,128,128]{2,1,0:T(8,128)(2,1)}, bf16[4,128,128]{2,1,0:T(8,128)(2,1)S(1)}, u32[]{:S(2)}, u32[]{:S(2)}) %collective-permute-start.21) | collective-permute-done | bytes 131104 | tf_op jit(solution)/shard_map/ppermute | solution.py:23
  147.7 8.7 %shard_map.109 = (f32[1,1024,128]{2,1,0:T(8,128)}, f32[1,512]{1,0:T(1,128)}) custom-call(s32[1]{0:T(128)} %bitcast.me_ref, s32[32]{0:T(128)} %bitcast.50, s32[1]{0:T(128)} %bitcast.23.live_ref, bf16[256,2048]{1,0:T(8,128)(2,1)} %shard_map.106.table_ref, s32[3,32,128]{2,1,0:T(8,128)} %bitcast.30, f32[1024,128]{1,0:T(8,128)} %shard_map.108.start_ref, ...), custom_call_target="tpu_custom_call" | custom-call | flops 4831838208 | bytes 1835008 | tf_op jit(solution)/shard_map/pallas_call | solution.py:197
  (87 shorter events, 22.5 us)
Async XLA Ops:
  2.0 32.8 %collective-permute-start.15 = (f32[4,512]{1,0:T(4,128)S(1)}, f32[4,512]{1,0:T(4,128)S(1)}, u32[]{:S(2)}, u32[]{:S(2)}) collective-permute-start(f32[4,512]{1,0:T(4,128)S(1)} %pad_maximum_fusion), channel_id=1, source_target_pairs={{1,0},{2,1},{3,2},{4,3},{5,4},{6,5},{7,6},{8,7},{9,8},{10,9},{11,1... | collective-permute-start | bytes 24584 | tf_op jit(solution)/shard_map/ppermute | solution.py:217
  3.3 37.2 %collective-permute-start.14 = (f32[4,512]{1,0:T(4,128)S(1)}, f32[4,512]{1,0:T(4,128)S(1)}, u32[]{:S(2)}, u32[]{:S(2)}) collective-permute-start(f32[4,512]{1,0:T(4,128)S(1)} %pad_maximum_fusion), channel_id=1, source_target_pairs={{0,1},{1,2},{2,3},{3,4},{4,5},{5,6},{6,7},{7,8},{8,9},{9,10},{10,1... | collective-permute-start | bytes 24584 | tf_op jit(solution)/shard_map/ppermute | solution.py:217
  6.4 36.5 %collective-permute-start.5 = (bf16[1024,128]{1,0:T(8,128)(2,1)}, bf16[1024,128]{1,0:T(8,128)(2,1)S(1)}, u32[]{:S(2)}, u32[]{:S(2)}) collective-permute-start(bf16[1024,128]{1,0:T(8,128)(2,1)} %bitcast.45), channel_id=1, source_target_pairs={{0,128},{32,160},{64,192},{96,224},{128,256},{160,288},{192,320},{... | collective-permute-start | bytes 786440 | tf_op jit(solution)/shard_map/ppermute | solution.py:23
  15.5 35.7 %collective-permute-start.4 = (bf16[1024,128]{1,0:T(8,128)(2,1)}, bf16[1024,128]{1,0:T(8,128)(2,1)S(1)}, u32[]{:S(2)}, u32[]{:S(2)}) collective-permute-start(bf16[1024,128]{1,0:T(8,128)(2,1)} %bitcast.46), channel_id=1, source_target_pairs={{0,896},{32,928},{64,960},{96,992},{128,0},{160,32},{192,64},{224,... | collective-permute-start | bytes 786440 | tf_op jit(solution)/shard_map/ppermute | solution.py:23
  28.9 32.8 %collective-permute-start.2 = (s32[4,128]{1,0:T(4,128)}, s32[4,128]{1,0:T(4,128)S(1)}, u32[]{:S(2)}, u32[]{:S(2)}) collective-permute-start(s32[4,128]{1,0:T(4,128)} %get-tuple-element.29), channel_id=1, source_target_pairs={{0,64},{32,96},{64,128},{96,160},{128,192},{160,224},{192,256},{22... | collective-permute-start | bytes 6152 | tf_op jit(solution)/shard_map/ppermute | solution.py:23
  34.8 28.8 %collective-permute-start.3 = (s32[4,128]{1,0:T(4,128)S(1)}, s32[4,128]{1,0:T(4,128)S(1)}, u32[]{:S(2)}, u32[]{:S(2)}) collective-permute-start(s32[4,128]{1,0:T(4,128)S(1)} %copy-done.24), channel_id=1, source_target_pairs={{0,960},{32,992},{64,0},{96,32},{128,64},{160,96},{192,128},{224,1... | collective-permute-start | bytes 6152 | tf_op jit(solution)/shard_map/ppermute | solution.py:23
  40.5 40.8 %collective-permute-start = (s32[8,128]{1,0:T(8,128)S(1)}, s32[8,128]{1,0:T(8,128)S(1)}, u32[]{:S(2)}, u32[]{:S(2)}) collective-permute-start(s32[8,128]{1,0:T(8,128)S(1)} %copy-done.20), channel_id=1, source_target_pairs={{0,32},{32,64},{64,96},{96,128},{128,160},{160,192},{192,224},{224... | collective-permute-start | bytes 12296 | tf_op jit(solution)/shard_map/ppermute | solution.py:23
  43.6 27.9 %collective-permute-start.8 = (bf16[512,128]{1,0:T(8,128)(2,1)S(1)}, bf16[512,128]{1,0:T(8,128)(2,1)S(1)}, u32[]{:S(2)}, u32[]{:S(2)}) collective-permute-start(bf16[512,128]{1,0:T(8,128)(2,1)S(1)} %get-tuple-element.56), channel_id=1, source_target_pairs={{0,128},{32,160},{64,192},{96,224},{128,256},{160,288},{192,320},{... | collective-permute-start | bytes 393224 | tf_op jit(solution)/shard_map/ppermute | solution.py:23
  51.8 21.6 %collective-permute-start.7 = (bf16[512,128]{1,0:T(8,128)(2,1)S(1)}, bf16[512,128]{1,0:T(8,128)(2,1)S(1)}, u32[]{:S(2)}, u32[]{:S(2)}) collective-permute-start(bf16[512,128]{1,0:T(8,128)(2,1)S(1)} %get-tuple-element.57), channel_id=1, source_target_pairs={{0,896},{32,928},{64,960},{96,992},{128,0},{160,32},{192,64},{224,... | collective-permute-start | bytes 393224 | tf_op jit(solution)/shard_map/ppermute | solution.py:23
  61.7 22.2 %collective-permute-start.9 = (bf16[512,128]{1,0:T(8,128)(2,1)S(1)}, bf16[512,128]{1,0:T(8,128)(2,1)S(1)}, u32[]{:S(2)}, u32[]{:S(2)}) collective-permute-start(bf16[512,128]{1,0:T(8,128)(2,1)S(1)} %get-tuple-element.55), channel_id=1, source_target_pairs={{0,128},{32,160},{64,192},{96,224},{128,256},{160,288},{192,320},{... | collective-permute-start | bytes 393224 | tf_op jit(solution)/shard_map/ppermute | solution.py:23
  63.6 28.0 %collective-permute-start.6 = (bf16[512,128]{1,0:T(8,128)(2,1)S(1)}, bf16[512,128]{1,0:T(8,128)(2,1)S(1)}, u32[]{:S(2)}, u32[]{:S(2)}) collective-permute-start(bf16[512,128]{1,0:T(8,128)(2,1)S(1)} %get-tuple-element.58), channel_id=1, source_target_pairs={{0,896},{32,928},{64,960},{96,992},{128,0},{160,32},{192,64},{224,... | collective-permute-start | bytes 393224 | tf_op jit(solution)/shard_map/ppermute | solution.py:23
  71.5 43.5 %copy-start.6 = (bf16[512,128]{1,0:T(8,128)(2,1)}, bf16[512,128]{1,0:T(8,128)(2,1)S(1)}, u32[]{:S(2)}) copy-start(bf16[512,128]{1,0:T(8,128)(2,1)S(1)} %collective-permute-done.8.refs_9_) | copy-start | bytes 393220
  71.5 22.2 %collective-permute-start.12 = (bf16[512,128]{1,0:T(8,128)(2,1)S(1)}, bf16[512,128]{1,0:T(8,128)(2,1)S(1)}, u32[]{:S(2)}, u32[]{:S(2)}) collective-permute-start(bf16[512,128]{1,0:T(8,128)(2,1)S(1)} %collective-permute-done.8.refs_9_), channel_id=1, source_target_pairs={{0,128},{32,160},{64,192},{96,224},{128,256},{160,288},{192,320},{... | collective-permute-start | bytes 393224 | tf_op jit(solution)/shard_map/ppermute | solution.py:23
  73.4 41.5 %copy-start.7 = (bf16[512,128]{1,0:T(8,128)(2,1)}, bf16[512,128]{1,0:T(8,128)(2,1)S(1)}, u32[]{:S(2)}) copy-start(bf16[512,128]{1,0:T(8,128)(2,1)S(1)} %collective-permute-done.7.refs_8_) | copy-start | bytes 393220
  73.4 29.3 %collective-permute-start.11 = (bf16[512,128]{1,0:T(8,128)(2,1)S(1)}, bf16[512,128]{1,0:T(8,128)(2,1)S(1)}, u32[]{:S(2)}, u32[]{:S(2)}) collective-permute-start(bf16[512,128]{1,0:T(8,128)(2,1)S(1)} %collective-permute-done.7.refs_8_), channel_id=1, source_target_pairs={{0,896},{32,928},{64,960},{96,992},{128,0},{160,32},{192,64},{224,... | collective-permute-start | bytes 393224 | tf_op jit(solution)/shard_map/ppermute | solution.py:23
  82.0 23.3 %collective-permute-start.1 = (s32[8,128]{1,0:T(8,128)S(1)}, s32[8,128]{1,0:T(8,128)S(1)}, u32[]{:S(2)}, u32[]{:S(2)}) collective-permute-start(s32[8,128]{1,0:T(8,128)S(1)} %copy-done.19), channel_id=1, source_target_pairs={{0,992},{32,0},{64,32},{96,64},{128,96},{160,128},{192,160},{224,1... | collective-permute-start | bytes 12296 | tf_op jit(solution)/shard_map/ppermute | solution.py:23
  83.9 21.4 %collective-permute-start.13 = (bf16[512,128]{1,0:T(8,128)(2,1)S(1)}, bf16[512,128]{1,0:T(8,128)(2,1)S(1)}, u32[]{:S(2)}, u32[]{:S(2)}) collective-permute-start(bf16[512,128]{1,0:T(8,128)(2,1)S(1)} %collective-permute-done.9.refs_10_), channel_id=1, source_target_pairs={{0,128},{32,160},{64,192},{96,224},{128,256},{160,288},{192,320},{... | collective-permute-start | bytes 393224 | tf_op jit(solution)/shard_map/ppermute | solution.py:23
  91.7 23.2 %collective-permute-start.10 = (bf16[512,128]{1,0:T(8,128)(2,1)S(1)}, bf16[512,128]{1,0:T(8,128)(2,1)S(1)}, u32[]{:S(2)}, u32[]{:S(2)}) collective-permute-start(bf16[512,128]{1,0:T(8,128)(2,1)S(1)} %collective-permute-done.6.refs_7_), channel_id=1, source_target_pairs={{0,896},{32,928},{64,960},{96,992},{128,0},{160,32},{192,64},{224,... | collective-permute-start | bytes 393224 | tf_op jit(solution)/shard_map/ppermute | solution.py:23
  93.7 25.9 %collective-permute-start.16 = (bf16[512,128]{1,0:T(8,128)(2,1)S(1)}, bf16[512,128]{1,0:T(8,128)(2,1)S(1)}, u32[]{:S(2)}, u32[]{:S(2)}) collective-permute-start(bf16[512,128]{1,0:T(8,128)(2,1)S(1)} %collective-permute-done.12.refs_13_), channel_id=1, source_target_pairs={{0,128},{32,160},{64,192},{96,224},{128,256},{160,288},{192,320},{... | collective-permute-start | bytes 393224 | tf_op jit(solution)/shard_map/ppermute | solution.py:23
  102.8 17.6 %collective-permute-start.17 = (bf16[512,128]{1,0:T(8,128)(2,1)S(1)}, bf16[512,128]{1,0:T(8,128)(2,1)S(1)}, u32[]{:S(2)}, u32[]{:S(2)}) collective-permute-start(bf16[512,128]{1,0:T(8,128)(2,1)S(1)} %collective-permute-done.11.refs_12_), channel_id=1, source_target_pairs={{0,896},{32,928},{64,960},{96,992},{128,0},{160,32},{192,64},{224,... | collective-permute-start | bytes 393224 | tf_op jit(solution)/shard_map/ppermute | solution.py:23
  123.7 23.2 %collective-permute-start.18 = (bf16[8,128,128]{2,1,0:T(8,128)(2,1)}, bf16[8,128,128]{2,1,0:T(8,128)(2,1)S(1)}, u32[]{:S(2)}, u32[]{:S(2)}) collective-permute-start(bf16[8,128,128]{2,1,0:T(8,128)(2,1)} %get-tuple-element.48), channel_id=1, source_target_pairs={{0,992},{32,0},{64,32},{96,64},{128,96},{160,128},{192,160},{224,1... | collective-permute-start | bytes 786440 | tf_op jit(solution)/shard_map/ppermute | solution.py:23
  127.4 19.5 %collective-permute-start.19 = (bf16[8,128,128]{2,1,0:T(8,128)(2,1)}, bf16[8,128,128]{2,1,0:T(8,128)(2,1)S(1)}, u32[]{:S(2)}, u32[]{:S(2)}) collective-permute-start(bf16[8,128,128]{2,1,0:T(8,128)(2,1)} %get-tuple-element.49), channel_id=1, source_target_pairs={{0,32},{32,64},{64,96},{96,128},{128,160},{160,192},{192,224},{224... | collective-permute-start | bytes 786440 | tf_op jit(solution)/shard_map/ppermute | solution.py:23
  129.6 14.1 %collective-permute-start.20 = (bf16[4,128,128]{2,1,0:T(8,128)(2,1)}, bf16[4,128,128]{2,1,0:T(8,128)(2,1)S(1)}, u32[]{:S(2)}, u32[]{:S(2)}) collective-permute-start(bf16[4,128,128]{2,1,0:T(8,128)(2,1)} %get-tuple-element.50), channel_id=1, source_target_pairs={{0,960},{32,992},{64,0},{96,32},{128,64},{160,96},{192,128},{224,1... | collective-permute-start | bytes 393224 | tf_op jit(solution)/shard_map/ppermute | solution.py:23
  136.8 10.1 %collective-permute-start.21 = (bf16[4,128,128]{2,1,0:T(8,128)(2,1)}, bf16[4,128,128]{2,1,0:T(8,128)(2,1)S(1)}, u32[]{:S(2)}, u32[]{:S(2)}) collective-permute-start(bf16[4,128,128]{2,1,0:T(8,128)(2,1)} %get-tuple-element.51), channel_id=1, source_target_pairs={{0,64},{32,96},{64,128},{96,160},{128,192},{160,224},{192,256},{22... | collective-permute-start | bytes 393224 | tf_op jit(solution)/shard_map/ppermute | solution.py:23
  (23 other events, 191.8 us)
